TPU v7x, 32 devices: a whole 2x2x4 slice. The times are simulated.
32 devices in a mesh: group: 16 (over z, y, core), tensor: 2 (over x).
Axes of the slice: x: 2, y: 2, z: 4, core: 2. Of those that a mesh axis runs over, the one named last changes fastest.
Arguments:
- turns: bfloat16 [16, 256, 4096], P('group', 'tensor'), may hold values from -16 to 16
- query_store: bfloat16 [16, 256, 4096], P('group', None, 'tensor'), may hold values from -0.09375 to 0.09375
- key_block_holder: bfloat16 [16, 256, 4, 128], P('group'), may hold values from -0.09375 to 0.09375
- value_block_holder: bfloat16 [16, 256, 4, 128], P('group'), may hold values from -0.09375 to 0.09375
- query_bias: float32 [4096], P('tensor'), may hold values from -3 to 3
- key_projection_bias: float32 [512], replicated, may hold values from -3 to 3
- value_projection_bias: float32 [512], replicated, may hold values from -3 to 3
- owner: int32 [16], replicated, may hold values from 0 to 15, each once
- lengths: int32 [16], P('group'), may hold values from 1 to 256, as said below
Outputs:
- attended: bfloat16 [16, 256, 4096], P('group', None, 'tensor')
Inputs may be any that keep to these rules, and one draw needn't show every extreme that they name: `owner`: each group index holds exactly one block. `lengths`: some group's turn fills all 256 positions.
All inputs are finite; a program needn't handle non-finite values.
Results may differ from a plain program's by a relative error of at most 0.0055.
The roundings to bfloat16 on the way count: a program that leaves them out, or rounds other values in their place, can miss the bound.
Values may be sent and summed in bfloat16 or wider, within the bound.
A program may use at most 128 MiB of HBM per device.

v0:
```python
import jax
import jax.numpy as jnp
from jax import lax
from jax.sharding import PartitionSpec as P

QUERY_HEADS = 32
KEY_VALUE_HEADS = 4
HEAD_SIZE = 128


rotary_base = 1000000.0


def rotary(heads, positions):
    half = heads.shape[-1] // 2
    expo = jnp.arange(half, dtype=jnp.float32) * 2.0 / heads.shape[-1]
    freqs = rotary_base ** (-expo)
    angles = positions[:, None] * freqs[None, :]
    cosine = jnp.cos(angles)[None]
    sine = jnp.sin(angles)[None]
    first = heads[..., :half]
    second = heads[..., half:]
    return jnp.concatenate(
        [first * cosine - second * sine, second * cosine + first * sine], axis=-1
    )


def per_device(
    turns,
    query_store,
    key_block_holder,
    value_block_holder,
    query_bias,
    key_projection_bias,
    value_projection_bias,
    owner,
    lengths,
):
    tensor_index = lax.axis_index("tensor")
    group_count = lax.axis_size("group")
    gathered = lax.all_gather(turns, "tensor", axis=1, tiled=True)[0]
    token_count = gathered.shape[0]
    block_rows = query_store.shape[1]
    query_cols = query_store.shape[2]
    heads_dev = query_cols // HEAD_SIZE
    query_per_key_head = QUERY_HEADS // KEY_VALUE_HEADS
    key_value_per_group = max(1, heads_dev // query_per_key_head)
    key_value_leading = tensor_index * heads_dev // query_per_key_head
    keys_mine = lax.dynamic_slice_in_dim(
        key_block_holder, key_value_leading, key_value_per_group, 2
    ).reshape(1, block_rows, key_value_per_group * HEAD_SIZE)
    values_mine = lax.dynamic_slice_in_dim(
        value_block_holder, key_value_leading, key_value_per_group, 2
    ).reshape(1, block_rows, key_value_per_group * HEAD_SIZE)
    inverse = (
        jnp.zeros((group_count,), jnp.int32).at[owner].set(jnp.arange(group_count, dtype=jnp.int32))
    )
    ordered = jnp.take(gathered.reshape(token_count, group_count, block_rows), inverse, axis=1)
    proj_query = jnp.einsum(
        "tgc,gcn->tn",
        ordered,
        lax.all_gather(query_store, "group", axis=0, tiled=True),
        preferred_element_type=jnp.float32,
    )
    proj_key = jnp.einsum(
        "tgc,gcn->tn",
        ordered,
        lax.all_gather(keys_mine, "group", axis=0, tiled=True),
        preferred_element_type=jnp.float32,
    )
    proj_value = jnp.einsum(
        "tgc,gcn->tn",
        ordered,
        lax.all_gather(values_mine, "group", axis=0, tiled=True),
        preferred_element_type=jnp.float32,
    )
    key_bias_rows = lax.dynamic_slice_in_dim(
        key_projection_bias.reshape(KEY_VALUE_HEADS, HEAD_SIZE),
        key_value_leading,
        key_value_per_group,
        0,
    ).reshape(key_value_per_group * HEAD_SIZE)
    bias_values = lax.dynamic_slice_in_dim(
        value_projection_bias.reshape(KEY_VALUE_HEADS, HEAD_SIZE),
        key_value_leading,
        key_value_per_group,
        0,
    ).reshape(key_value_per_group * HEAD_SIZE)
    positions = jnp.arange(token_count, dtype=jnp.float32)
    raw_query = (
        (proj_query + query_bias).reshape(token_count, heads_dev, HEAD_SIZE).transpose(1, 0, 2)
    )
    unbiased_key = (
        (proj_key + key_bias_rows)
        .reshape(token_count, key_value_per_group, HEAD_SIZE)
        .transpose(1, 0, 2)
    )
    unbiased_value = (
        (proj_value + bias_values)
        .reshape(token_count, key_value_per_group, HEAD_SIZE)
        .transpose(1, 0, 2)
    )
    queries = rotary(raw_query, positions).astype(jnp.bfloat16)
    keys_rot = rotary(unbiased_key, positions).astype(jnp.bfloat16)
    values_cast = unbiased_value.astype(jnp.bfloat16)
    repeat_count = heads_dev // key_value_per_group
    keys_full = jnp.repeat(keys_rot, repeat_count, axis=0)
    values_full = jnp.repeat(values_cast, repeat_count, axis=0)
    index = jnp.arange(token_count, dtype=jnp.int32)
    span = min(256, token_count)
    outputs = []
    for block in range(token_count // span):
        first = block * span
        last = first + span
        scores = jnp.einsum(
            "htd,hsd->hts",
            queries[:, first:last],
            keys_full[:, :last],
            preferred_element_type=jnp.float32,
        ) * HEAD_SIZE ** (-0.5)
        causal = index[None, :last] <= index[first:last, None]
        scores = jnp.where(causal[None], scores, -jnp.inf)
        top = jnp.max(scores, axis=-1, keepdims=True)
        expd = jnp.exp(scores - top)
        weights = (expd / jnp.sum(expd, axis=-1, keepdims=True)).astype(jnp.bfloat16)
        outputs.append(
            jnp.einsum(
                "hts,hsd->htd", weights, values_full[:, :last], preferred_element_type=jnp.float32
            )
        )
    mixed = jnp.concatenate(outputs, axis=1)
    mixed = mixed.transpose(1, 0, 2).reshape(token_count, query_cols)
    live = (index < lengths[0])[:, None]
    return jnp.where(live, mixed, 0.0).astype(jnp.bfloat16)[None]


def solution(mesh):
    in_specs = (
        P("group", "tensor", None),
        P("group", None, "tensor"),
        P("group", None, None, None),
        P("group", None, None, None),
        P("tensor"),
        P(),
        P(),
        P(),
        P("group"),
    )
    out_specs = P("group", None, "tensor")
    return jax.shard_map(
        per_device, mesh=mesh, in_specs=in_specs, out_specs=out_specs, check_vma=False
    )
```

profile of v0, /device:TPU:0, one launch (start us, length us, event | category | flops | bytes accessed | tf_op | source)
XLA Modules:
  0.0 279.1 jit_solution(3044673311815273729)
XLA Ops:
  6.5 0.0 copy-start
  6.5 0.0 copy-start.3
  6.5 0.0 copy-start.2
  6.5 0.0 all-gather.5.cloned.1.call-start
  6.5 2.3 copy.46
  8.9 0.0 copy-start.6
  8.9 0.0 copy-start.4
  8.9 0.0 all-gather.5.cloned.1.call-update
  8.9 0.0 all-gather.9.cloned.1.call-start
  9.0 0.0 copy-done.3
  9.0 0.0 copy-done.2
  9.0 0.3 constant_dynamic-slice_fusion
  9.3 0.1 copy.64
  9.4 0.8 copy.50
  10.2 0.0 all-gather.9.cloned.1.call-update
  10.2 0.0 all-gather.11.cloned.1.call-start
  10.2 0.1 copy.63
  10.4 0.8 copy.56
  11.1 0.0 all-gather.11.cloned.1.call-update
  11.1 0.0 all-gather.7.cloned.1.call-start
  11.2 0.5 all-gather.7.cloned.1.call-update
  11.7 0.5 fusion.35
  12.2 0.1 copy.52
  12.3 0.1 copy.53
  13.1 0.0 copy-done.6
  13.1 0.6 scatter_custom_fusion
  13.7 0.0 copy-done
  13.8 0.0 copy-done.4
  13.9 31.0 %all-gather.5.cloned.1.call-done = bf16[1,256,4096]{1,2,0:T(8,128)(2,1)} async-done(((bf16[1,128,4096]{1,2,0:T(8,128)(2,1)}), bf16[1,256,4096]{1,2,0:T(8,128)(2,1)}) %all-gather.5.cloned.1.call-update) | async-done | bytes 2097168 | tf_op jit(solution)/shard_map/all_gather | solution.py:41
  44.8 2.8 %copy.47 = bf16[256,16,256]{2,0,1:T(8,128)(2,1)S(1)} copy(bf16[256,16,256]{0,2,1:T(8,128)(2,1)} %bitcast.73) | data formatting | bytes 4194304 | tf_op jit(solution)/shard_map/reshape;squeeze | solution.py:58
  47.7 2.0 gather_fusion
  49.7 0.0 copy-start.1
  49.7 38.7 %all-gather.9.cloned.1.call-done = bf16[16,256,256]{2,1,0:T(8,128)(2,1)} async-done(((bf16[1,256,256]{2,1,0:T(8,128)(2,1)}), bf16[16,256,256]{2,1,0:T(8,128)(2,1)}) %all-gather.9.cloned.1.call-update) | async-done | bytes 2097168 | tf_op jit(solution)/shard_map/all_gather | solution.py:68
  88.4 3.2 %fusion.24 = f32[256,256]{0,1:T(8,128)S(1)} fusion(bf16[16,256,256]{2,1,0:T(8,128)(2,1)} %all-gather.9.cloned.1.call-done, f32[256]{0:T(256)S(1)} %dynamic-slice_bitcast_fusion.1, bf16[16,256,256]{2,1,0:T(8,128)(2,1)} %gather_fusion, pred[16]{0:T(512)(128)(4,1)S(1)} %compare_and_fusion), kind=kOutput, calls=%fused_computation.27 | convolution fusion | flops 537985024 | bytes 4457488 | tf_op jit(solution)/shard_map/tgc,gcn->tn/dot_general | solution.py:65
  91.7 0.1 copy.54
  91.9 0.0 copy-start.5
  91.9 38.9 %all-gather.11.cloned.1.call-done = bf16[16,256,256]{2,1,0:T(8,128)(2,1)} async-done(((bf16[1,256,256]{2,1,0:T(8,128)(2,1)}), bf16[16,256,256]{2,1,0:T(8,128)(2,1)}) %all-gather.11.cloned.1.call-update) | async-done | bytes 2097168 | tf_op jit(solution)/shard_map/all_gather | solution.py:74
  130.8 0.0 copy-done.1
  130.8 2.7 fusion.27
  133.5 125.1 %all-gather.7.cloned.1.call-done = bf16[16,256,2048]{2,1,0:T(8,128)(2,1)} async-done(((bf16[1,256,2048]{2,1,0:T(8,128)(2,1)}), bf16[16,256,2048]{2,1,0:T(8,128)(2,1)}) %all-gather.7.cloned.1.call-update) | async-done | bytes 16777232 | tf_op jit(solution)/shard_map/all_gather | solution.py:62
  258.5 0.0 copy-done.5
  258.5 8.2 %fusion.12 = f32[32,16,8,128]{3,2,1,0:T(8,128)S(1)} fusion(bf16[16,256,2048]{2,1,0:T(8,128)(2,1)} %all-gather.7.cloned.1.call-done, f32[2048]{0:T(1024)S(1)} %copy-done.5, bf16[16,256,256]{2,1,0:T(8,128)(2,1)S(1)} %copy-done.1, pred[16]{0:T(512)(128)(4,1)S(1)} %compare_and_fusion), kind=kOutput, calls=%fused_computation.23 | convolution fusion | flops 4296540160 | bytes 20979728 | tf_op jit(solution)/shard_map/tgc,gcn->tn/dot_general | solution.py:59
  266.8 0.2 copy.67
  267.0 0.8 subtract_convert_fusion
  267.8 0.2 broadcast_in_dim.67
  268.0 0.8 fusion.30
  268.8 1.2 fusion.41
  270.0 0.1 broadcast_in_dim.69
  270.1 0.6 fusion.10
  270.7 0.6 copy.59
  271.3 1.2 select_convert_fusion
  (12 shorter events, 0.1 us)
Async XLA Ops:
  6.5 7.2 %copy-start = (f32[512]{0:T(512)S(1)}, f32[512]{0:T(512)}, u32[]{:S(2)}) copy-start(f32[512]{0:T(512)} %param.14) | copy-start | bytes 6148
  6.5 2.4 copy-start.3
  6.5 2.4 copy-start.2
  6.5 38.3 %all-gather.5.cloned.1.call-start = ((), (), s32[]{:S(2)}) async-start(), calls=%async_computation | async-start | bytes 3145728 | tf_op jit(solution)/shard_map/all_gather | solution.py:41
  8.9 4.2 %copy-start.6 = (s32[16]{0:T(128)S(1)}, s32[16]{0:T(128)}, u32[]{:S(2)}) copy-start(s32[16]{0:T(128)} %param.16) | copy-start | bytes 196
  8.9 4.9 %copy-start.4 = (f32[512]{0:T(512)S(1)}, f32[512]{0:T(512)}, u32[]{:S(2)}) copy-start(f32[512]{0:T(512)} %param.15) | copy-start | bytes 6148
  8.9 79.5 %all-gather.9.cloned.1.call-start = ((), (), s32[]{:S(2)}) async-start(), calls=%async_computation.2 | async-start | bytes 2228224 | tf_op jit(solution)/shard_map/all_gather | solution.py:68
  10.2 120.6 %all-gather.11.cloned.1.call-start = ((), (), s32[]{:S(2)}) async-start(), calls=%async_computation.3 | async-start | bytes 2228224 | tf_op jit(solution)/shard_map/all_gather | solution.py:74
  11.1 247.4 %all-gather.7.cloned.1.call-start = ((), (), s32[]{:S(2)}) async-start(), calls=%async_computation.1 | async-start | bytes 17825792 | tf_op jit(solution)/shard_map/all_gather | solution.py:62
  49.7 81.1 %copy-start.1 = (bf16[16,256,256]{2,1,0:T(8,128)(2,1)S(1)}, bf16[16,256,256]{2,1,0:T(8,128)(2,1)}, u32[]{:S(2)}) copy-start(bf16[16,256,256]{2,1,0:T(8,128)(2,1)} %gather_fusion) | copy-start | bytes 6291460
  91.9 166.7 %copy-start.5 = (f32[2048]{0:T(1024)S(1)}, f32[2048]{0:T(1024)}, u32[]{:S(2)}) copy-start(f32[2048]{0:T(1024)} %param.13) | copy-start | bytes 24580
Sparse Core Ops, SparseCore 0:
  9.0 35.7 all-gather.4
  47.0 41.3 all-gather.8
  90.6 40.1 all-gather.10
  132.8 125.6 all-gather.6
where the time goes:
time: 279 us
  waiting for transfers between devices  234 us (84%)
  matrix products  15.5 us (6%)
  between operations  14.1 us (5%)
  local copies, waits for them, and re-layouts  11.3 us (4%)
  other arithmetic  3.83 us (1%)
    all_gather x1, waiting for transfers between devices, per_device(): lax.all_gather(query_store, 'group', axis=0, tiled=True)  125 us
    all_gather x1, waiting for transfers between devices, per_device(): lax.all_gather(values_mine, 'group', axis=0, tiled=True)  38.9 us
    all_gather x1, waiting for transfers between devices, per_device(): lax.all_gather(keys_mine, 'group', axis=0, tiled=True)  38.7 us
    all_gather x1, waiting for transfers between devices, per_device(): gathered = lax.all_gather(turns, 'tensor', axis=1, tiled=True)[0]  31 us
    dot_general x1, matrix products, per_device(): jnp.einsum('tgc,gcn->tn', ordered, lax.all_gather(query_store, 'group', a...  8.24 us
  transfers between devices with their start and end apart: 4, of which 4 were waited for; matrix products, arithmetic and copies ran while one was open for 5% of the time, Pallas kernels for 0%

commit v1 on v0

--- a/solution.py
+++ b/solution.py
@@ -1,6 +1,9 @@
 import jax
 import jax.numpy as jnp
+import numpy as np
 from jax import lax
+from jax.experimental import pallas as pl
+from jax.experimental.pallas import tpu as pltpu
 from jax.sharding import PartitionSpec as P
 
 QUERY_HEADS = 32
@@ -55,7 +58,13 @@
     inverse = (
         jnp.zeros((group_count,), jnp.int32).at[owner].set(jnp.arange(group_count, dtype=jnp.int32))
     )
-    ordered = jnp.take(gathered.reshape(token_count, group_count, block_rows), inverse, axis=1)
+    ordered = jnp.stack(
+        [
+            lax.dynamic_slice_in_dim(gathered, inverse[holder] * block_rows, block_rows, 1)
+            for holder in range(group_count)
+        ],
+        axis=1,
+    )
     proj_query = jnp.einsum(
         "tgc,gcn->tn",
         ordered,
@@ -134,6 +143,363 @@
     return jnp.where(live, mixed, 0.0).astype(jnp.bfloat16)[None]
 
 
+RING = 8
+BLOCKS = 16
+ROWS = 256
+TOKENS = 256
+WIDTH_A = 768
+WIDTH_B = 512
+MESH = pl.DeviceIdType.MESH
+
+
+def group_of(place, core):
+    y = place // 4
+    z = place + y * (7 - 2 * place)
+    return z * 4 + y * 2 + core
+
+
+def ring_kernel(
+    row_block_ref,
+    length_ref,
+    turns_ref,
+    store_ref,
+    kv_ref,
+    query_bias_ref,
+    key_bias_ref,
+    value_bias_ref,
+    cosine_ref,
+    sine_ref,
+    out_ref,
+    x_ref,
+    wa_ref,
+    wb_ref,
+    acca_ref,
+    accb_ref,
+    keys_ref,
+    values_ref,
+    local_sem,
+    x_local,
+    x_send,
+    x_recv,
+    ring_send,
+    ring_recv,
+    sib_send,
+    sib_recv,
+):
+    g = lax.axis_index("group")
+    t = lax.axis_index("tensor")
+    core = lax.rem(g, 2)
+    y = lax.rem(g // 2, 2)
+    z = g // 4
+    r = z + y * (7 - 2 * z)
+    other = 1 - core
+    onward = (group_of(lax.rem(r + 1, RING), core), group_of(lax.rem(r + RING - 1, RING), core))
+    sibling = g + 1 - 2 * core
+    half = TOKENS // 2
+    weights = (wa_ref, wb_ref)
+    accs = (acca_ref, accb_ref)
+
+    mine = pl.ds(pl.multiple_of(t * half, half), half)
+    x_loads = [
+        pltpu.make_async_copy(
+            turns_ref.at[0, :, b * ROWS : b * ROWS + ROWS], x_ref.at[b, mine], x_local.at[b]
+        )
+        for b in range(BLOCKS)
+    ]
+    loads = []
+    for d in range(2):
+        loads.append(
+            pltpu.make_async_copy(
+                kv_ref.at[:, d * 256 : d * 256 + 256],
+                wa_ref.at[core, r, d, :, 0:256],
+                local_sem.at[3 * d],
+            )
+        )
+        loads.append(
+            pltpu.make_async_copy(
+                store_ref.at[0, :, d * 1024 : d * 1024 + 512],
+                wa_ref.at[core, r, d, :, 256:768],
+                local_sem.at[1 + 3 * d],
+            )
+        )
+        loads.append(
+            pltpu.make_async_copy(
+                store_ref.at[0, :, d * 1024 + 512 : d * 1024 + 1024],
+                wb_ref.at[core, r, d],
+                local_sem.at[2 + 3 * d],
+            )
+        )
+    for load in loads + x_loads:
+        load.start()
+
+    barrier = pltpu.get_barrier_semaphore()
+    for partner in ((onward[0], t), (onward[1], t), (sibling, t), (g, 1 - t)):
+        pl.semaphore_signal(barrier, inc=1, device_id=partner, device_id_type=MESH)
+    pl.semaphore_wait(barrier, 4)
+
+    def came_from(d, j):
+        return lax.rem(r + RING - j, RING) if d == 0 else lax.rem(r + j, RING)
+
+    def ring_copy(d, u, s):
+        slot = weights[u].at[core, came_from(d, s), d]
+        return pltpu.make_async_remote_copy(
+            src_ref=slot,
+            dst_ref=slot,
+            send_sem=ring_send.at[d, u, s],
+            recv_sem=ring_recv.at[d, u, s],
+            device_id=(onward[d], t),
+            device_id_type=MESH,
+        )
+
+    def ring_arrival(d, u, s):
+        slot = weights[u].at[core, came_from(d, s + 1), d]
+        return pltpu.make_async_remote_copy(
+            src_ref=slot,
+            dst_ref=slot,
+            send_sem=ring_send.at[d, u, s],
+            recv_sem=ring_recv.at[d, u, s],
+            device_id=(onward[d], t),
+            device_id_type=MESH,
+        )
+
+    def sib_copy(d, u, j):
+        slot = weights[u].at[core, came_from(d, j), d]
+        return pltpu.make_async_remote_copy(
+            src_ref=slot,
+            dst_ref=slot,
+            send_sem=sib_send.at[d, u, j],
+            recv_sem=sib_recv.at[d, u, j],
+            device_id=(sibling, t),
+            device_id_type=MESH,
+        )
+
+    def sib_arrival(d, u, j):
+        slot = weights[u].at[other, came_from(d, j), d]
+        return pltpu.make_async_remote_copy(
+            src_ref=slot,
+            dst_ref=slot,
+            send_sem=sib_send.at[d, u, j],
+            recv_sem=sib_recv.at[d, u, j],
+            device_id=(sibling, t),
+            device_id_type=MESH,
+        )
+
+    x_copy = pltpu.make_async_remote_copy(
+        src_ref=x_ref.at[:, mine],
+        dst_ref=x_ref.at[:, mine],
+        send_sem=x_send,
+        recv_sem=x_recv,
+        device_id=(g, 1 - t),
+        device_id_type=MESH,
+    )
+
+    for load in loads:
+        load.wait()
+    for u in range(2):
+        for d in range(2):
+            ring_copy(d, u, 0).start()
+    for load in x_loads:
+        load.wait()
+    x_copy.start()
+    for u in range(2):
+        for d in range(2):
+            sib_copy(d, u, 0).start()
+
+    for d in range(2):
+        head = pl.ds(pl.multiple_of((2 * t + d) * HEAD_SIZE, HEAD_SIZE), HEAD_SIZE)
+        acca_ref[d, :, 0:128] = jnp.broadcast_to(key_bias_ref[:, head], (TOKENS, 128))
+        acca_ref[d, :, 128:256] = jnp.broadcast_to(value_bias_ref[:, head], (TOKENS, 128))
+        acca_ref[d, :, 256:768] = jnp.broadcast_to(
+            query_bias_ref[:, d * 1024 : d * 1024 + 512], (TOKENS, 512)
+        )
+        accb_ref[d] = jnp.broadcast_to(
+            query_bias_ref[:, d * 1024 + 512 : d * 1024 + 1024], (TOKENS, 512)
+        )
+
+    def add_product(u, d, place, which):
+        holder = group_of(place, which)
+        block = x_ref[row_block_ref[holder]]
+        accs[u][d] += jnp.dot(
+            block, weights[u][which, place, d], preferred_element_type=jnp.float32
+        )
+
+    def use_own(j):
+        for u in range(2):
+            for d in range(2):
+                add_product(u, d, came_from(d, j), core)
+
+    def use_sibling(j):
+        for u in range(2):
+            for d in range(2):
+                sib_arrival(d, u, j).wait_recv()
+                add_product(u, d, came_from(d, j), other)
+
+    def step(s, carry):
+        for u in range(2):
+            for d in range(2):
+                ring_arrival(d, u, s).wait_recv()
+
+                @pl.when(s < RING - 2)
+                def _():
+                    ring_copy(d, u, s + 1).start()
+
+                sib_copy(d, u, s + 1).start()
+
+        @pl.when(s == 0)
+        def _():
+            x_copy.wait_recv()
+
+        use_own(s)
+        use_sibling(s)
+        return carry
+
+    lax.fori_loop(0, RING - 1, step, 0)
+    use_own(RING - 1)
+    use_sibling(RING - 1)
+
+    def rotate(raw):
+        return (raw * cosine_ref[...] + pltpu.roll(raw, 64, 1) * sine_ref[...]).astype(jnp.bfloat16)
+
+    for d in range(2):
+        keys_ref[d] = rotate(acca_ref[d, :, 0:128])
+        values_ref[d] = acca_ref[d, :, 128:256].astype(jnp.bfloat16)
+
+    length = length_ref[0]
+    scale = HEAD_SIZE ** (-0.5)
+
+    def attend(raw, d):
+        query = rotate(raw)
+        parts = []
+        for piece in range(2):
+            low, high = piece * half, piece * half + half
+            scores = (
+                lax.dot_general(
+                    query[low:high],
+                    keys_ref[d, 0:high],
+                    (((1,), (1,)), ((), ())),
+                    preferred_element_type=jnp.float32,
+                )
+                * scale
+            )
+            rows = lax.broadcasted_iota(jnp.int32, (half, high), 0) + low
+            cols = lax.broadcasted_iota(jnp.int32, (half, high), 1)
+            scores = jnp.where(cols <= rows, scores, -jnp.inf)
+            top = jnp.max(scores, axis=-1, keepdims=True)
+            expd = jnp.exp(scores - top)
+            total = jnp.sum(expd, axis=-1, keepdims=True)
+            shares = (expd / total).astype(jnp.bfloat16)
+            mixed = jnp.dot(shares, values_ref[d, 0:high], preferred_element_type=jnp.float32)
+            live = lax.broadcasted_iota(jnp.int32, (half, HEAD_SIZE), 0) + low < length
+            parts.append(jnp.where(live, mixed, 0.0).astype(jnp.bfloat16))
+        return parts
+
+    def head_step(h, carry):
+        lane = pl.multiple_of(h * HEAD_SIZE, HEAD_SIZE)
+        for d in range(2):
+            for u in range(2):
+                start = 256 if u == 0 else 0
+                raw = accs[u][d, :, pl.ds(start + lane, HEAD_SIZE)]
+                to = pl.ds(d * 1024 + u * 512 + lane, HEAD_SIZE)
+                parts = attend(raw, d)
+                for piece in range(2):
+                    out_ref[0, piece * half : piece * half + half, to] = parts[piece]
+        return carry
+
+    lax.fori_loop(0, 4, head_step, 0)
+
+    x_copy.wait_send()
+
+    def drain(s, carry):
+        for u in range(2):
+            for d in range(2):
+                ring_copy(d, u, s).wait_send()
+                sib_copy(d, u, s).wait_send()
+        return carry
+
+    lax.fori_loop(0, RING - 1, drain, 0)
+    for u in range(2):
+        for d in range(2):
+            sib_copy(d, u, RING - 1).wait_send()
+
+
+def rotary_tables():
+    freqs = rotary_base ** (-2.0 * np.arange(64) / HEAD_SIZE)
+    angles = np.arange(TOKENS)[:, None] * freqs[None, :]
+    cosine, sine = np.cos(angles), np.sin(angles)
+    return (
+        np.concatenate([cosine, cosine], axis=1).astype(np.float32),
+        np.concatenate([-sine, sine], axis=1).astype(np.float32),
+    )
+
+
+def per_device_ring(
+    turns,
+    query_store,
+    key_block_holder,
+    value_block_holder,
+    query_bias,
+    key_projection_bias,
+    value_projection_bias,
+    owner,
+    lengths,
+):
+    t = lax.axis_index("tensor")
+    keys_mine = lax.dynamic_slice_in_dim(key_block_holder[0], 2 * t, 2, 1)
+    values_mine = lax.dynamic_slice_in_dim(value_block_holder[0], 2 * t, 2, 1)
+    kv = jnp.concatenate([keys_mine, values_mine], axis=2).reshape(ROWS, 512)
+    numbers = jnp.arange(BLOCKS, dtype=jnp.int32)
+    row_block = jnp.sum(
+        jnp.where(owner[None, :] == numbers[:, None], numbers[None, :], 0), axis=1, dtype=jnp.int32
+    )
+    cosine, sine = rotary_tables()
+    smem = pl.BlockSpec(memory_space=pltpu.SMEM)
+    vmem = pl.BlockSpec(memory_space=pltpu.VMEM)
+    hbm = pl.BlockSpec(memory_space=pl.ANY)
+    return pl.pallas_call(
+        ring_kernel,
+        out_shape=jax.ShapeDtypeStruct((1, TOKENS, 2048), jnp.bfloat16),
+        in_specs=[smem, smem, hbm, hbm, hbm, vmem, vmem, vmem, vmem, vmem],
+        out_specs=vmem,
+        scratch_shapes=[
+            pltpu.VMEM((BLOCKS, TOKENS, ROWS), jnp.bfloat16),
+            pltpu.VMEM((2, RING, 2, ROWS, WIDTH_A), jnp.bfloat16),
+            pltpu.VMEM((2, RING, 2, ROWS, WIDTH_B), jnp.bfloat16),
+            pltpu.VMEM((2, TOKENS, WIDTH_A), jnp.float32),
+            pltpu.VMEM((2, TOKENS, WIDTH_B), jnp.float32),
+            pltpu.VMEM((2, TOKENS, HEAD_SIZE), jnp.bfloat16),
+            pltpu.VMEM((2, TOKENS, HEAD_SIZE), jnp.bfloat16),
+            pltpu.SemaphoreType.DMA((6,)),
+            pltpu.SemaphoreType.DMA((BLOCKS,)),
+            pltpu.SemaphoreType.DMA,
+            pltpu.SemaphoreType.DMA,
+            pltpu.SemaphoreType.DMA((2, 2, RING - 1)),
+            pltpu.SemaphoreType.DMA((2, 2, RING - 1)),
+            pltpu.SemaphoreType.DMA((2, 2, RING)),
+            pltpu.SemaphoreType.DMA((2, 2, RING)),
+        ],
+        compiler_params=pltpu.CompilerParams(
+            collective_id=0, has_side_effects=True, vmem_limit_bytes=48 * 1024 * 1024
+        ),
+    )(
+        row_block,
+        lengths,
+        turns,
+        query_store,
+        kv,
+        query_bias[None],
+        key_projection_bias[None],
+        value_projection_bias[None],
+        jnp.asarray(cosine),
+        jnp.asarray(sine),
+    )
+
+
+def pick(turns, *rest):
+    fits = lax.axis_size("group") == 16 and lax.axis_size("tensor") == 2
+    fits = fits and turns.shape[1:] == (128, 4096)
+    return per_device_ring(turns, *rest) if fits else per_device(turns, *rest)
+
+
 def solution(mesh):
     in_specs = (
         P("group", "tensor", None),
@@ -148,5 +514,5 @@
     )
     out_specs = P("group", None, "tensor")
     return jax.shard_map(
-        per_device, mesh=mesh, in_specs=in_specs, out_specs=out_specs, check_vma=False
-    )
+        pick, mesh=mesh, in_specs=in_specs, out_specs=out_specs, check_vma=False
+    )

time: 279 us -> 123 us (0.44)
  waiting for transfers between devices: 234 us -> 0 us
  Pallas kernels: 0 us -> 116 us
  matrix products: 15.5 us -> 0 us
  between operations: 14.1 us -> 0.82 us
  local copies, waits for them, and re-layouts: 11.3 us -> 4.43 us
  other arithmetic: 3.83 us -> 1.04 us
    all_gather x4 -> x0, waiting for transfers between devices: 234 us -> none  [the longest x1 125 us: per_device(): lax.all_gather(query_store, 'group', axis=0, tiled=True)]
    pallas_call x0 -> x1, Pallas kernels: none -> 116 us  [per_device_ring(): pl.pallas_call(ring_kernel, out_shape=jax.ShapeDtypeStruct((1, TOKENS, 20...]
    dot_general x5 -> x0, matrix products: 15.5 us -> none  [the longest x1 8.24 us: per_device(): jnp.einsum('tgc,gcn->tn', ordered, lax.all_gather(query_store, 'group', a...]
    another operation x1 -> x0, local copies, waits for them, and re-layouts: 2.85 us -> none  [per_device(): gathered.reshape(token_count, group_count, block_rows)]
  transfers between devices with their start and end apart: 4 -> 0, of which waited for: 4 -> 0; matrix products, arithmetic and copies ran while one was open for 5% -> 0% of each run, Pallas kernels for 0% -> 0%
where the time goes in v1:
time: 123 us
  Pallas kernels  116 us (94%)
  local copies, waits for them, and re-layouts  4.43 us (4%)
    pallas_call x1, Pallas kernels, per_device_ring(): pl.pallas_call(ring_kernel, out_shape=jax.ShapeDtypeStruct((1, TOKENS, 20...  116 us
    unnamed x16, local copies, waits for them, and re-layouts  3.12 us

profile of v1, /device:TPU:0, one launch (start us, length us, event | category | flops | bytes accessed | tf_op | source)
XLA Modules:
  0.0 122.8 jit_solution(11140901433991322533)
XLA Ops:
  0.0 0.0 copy-start
  0.7 0.8 select_reduce_fusion.row_block_ref
  1.5 1.3 %dynamic-slice_bitcast_fusion = (bf16[256,2,128]{2,1,0:T(2,128)(2,1)S(1)}, bf16[256,2,128]{2,1,0:T(2,128)(2,1)S(1)}) fusion(bf16[1,256,4,128]{3,2,1,0:T(4,128)(2,1)} %param.14, s32[]{:T(128)S(6)} %select_n.9, bf16[1,256,4,128]{3,2,1,0:T(4,128)(2,1)} %param.13), kind=kLoop, calls=%fused_computation.1 | loop fusion | bytes 524292 | tf_op jit(solution)/shard_map/dynamic_slice | solution.py:448
  2.8 0.3 pad_maximum_fusion
  3.1 0.0 copy-start.2
  3.1 0.0 copy-start.3
  3.1 0.0 copy-start.4
  3.1 0.0 copy-start.5
  3.2 0.0 copy-start.6
  3.2 0.0 copy-done
  3.2 0.8 copy-done.2
  4.0 0.1 copy-done.3
  4.1 0.0 copy-done.4
  4.1 0.0 copy-done.5
  4.1 0.0 copy-done.6
  4.1 0.0 copy-start.1
  4.1 1.2 copy-done.1
  5.3 116.5 %shard_map.109 = bf16[1,256,2048]{2,1,0:T(8,128)(2,1)S(1)} custom-call(s32[16]{0:T(128)S(1)} %select_reduce_fusion.row_block_ref, s32[1]{0:T(128)S(6)} %copy.14.length_ref, bf16[1,128,4096]{2,1,0:T(8,128)(2,1)S(1)} %copy-done, bf16[1,256,2048]{2,1,0:T(8,128)(2,1)S(1)} %copy-done.1, bf16[256,512]{1,0:T(8,128)(2,1)S(1)} %bitcast.9, f32[1,2048]{1,0:T(1,128)S(1)} %bitcast.10, ...), custom_call_target="tpu_custom_call" | custom-call | tf_op jit(solution)/shard_map/pallas_call | solution.py:458
  121.8 1.0 copy.15
  (1 shorter events, 0.0 us)
Async XLA Ops:
  0.0 3.2 %copy-start = (bf16[1,128,4096]{2,1,0:T(8,128)(2,1)S(1)}, bf16[1,128,4096]{2,1,0:T(8,128)(2,1)}, u32[]{:S(2)}) copy-start(bf16[1,128,4096]{2,1,0:T(8,128)(2,1)} %turns_ref.1) | copy-start | bytes 3145732
  3.1 0.9 copy-start.2
  3.1 1.0 copy-start.3
  3.1 1.0 copy-start.4
  3.1 0.9 copy-start.5
  3.2 0.9 copy-start.6
  4.1 1.2 copy-start.1

commit v2 on v0

--- a/solution.py
+++ b/solution.py
@@ -1,6 +1,9 @@
 import jax
 import jax.numpy as jnp
+import numpy as np
 from jax import lax
+from jax.experimental import pallas as pl
+from jax.experimental.pallas import tpu as pltpu
 from jax.sharding import PartitionSpec as P
 
 QUERY_HEADS = 32
@@ -55,7 +58,13 @@
     inverse = (
         jnp.zeros((group_count,), jnp.int32).at[owner].set(jnp.arange(group_count, dtype=jnp.int32))
     )
-    ordered = jnp.take(gathered.reshape(token_count, group_count, block_rows), inverse, axis=1)
+    ordered = jnp.stack(
+        [
+            lax.dynamic_slice_in_dim(gathered, inverse[holder] * block_rows, block_rows, 1)
+            for holder in range(group_count)
+        ],
+        axis=1,
+    )
     proj_query = jnp.einsum(
         "tgc,gcn->tn",
         ordered,
@@ -134,6 +143,442 @@
     return jnp.where(live, mixed, 0.0).astype(jnp.bfloat16)[None]
 
 
+BLOCKS = 16
+ROWS = 256
+TOKENS = 256
+HALF = 128
+LAYERS = 4
+WIDTHS = (768, 512)
+MESH = pl.DeviceIdType.MESH
+
+
+def plane_kernel(
+    row_block_ref,
+    length_ref,
+    turns_ref,
+    store_ref,
+    kv_ref,
+    query_bias_ref,
+    key_bias_ref,
+    value_bias_ref,
+    cosine_ref,
+    sine_ref,
+    out_ref,
+    x_ref,
+    wa_ref,
+    wb_ref,
+    acca_ref,
+    accb_ref,
+    keys_ref,
+    values_ref,
+    back_ref,
+    local_sem,
+    x_local,
+    x_send,
+    x_recv,
+    y_send,
+    y_recv,
+    z_send,
+    z_recv,
+    sib_send,
+    sib_recv,
+    back_send,
+    back_recv,
+):
+    g = lax.axis_index("group")
+    t = lax.axis_index("tensor")
+    core = lax.rem(g, 2)
+    y = lax.rem(g // 2, 2)
+    z = g // 4
+    other = 1 - core
+    across = g + 2 - 4 * y
+    sibling = g + 1 - 2 * core
+    weights = (wa_ref, wb_ref)
+    accs = (acca_ref, accb_ref)
+
+    def pieces(d):
+        first = pl.multiple_of(d * 1024, 1024)
+        second = pl.multiple_of(d * 1024 + 512, 512)
+        return (
+            (kv_ref.at[:, pl.ds(pl.multiple_of(d * 256, 256), 256)], wa_ref.at[core, z, y, :, 0:256]),
+            (store_ref.at[0, :, pl.ds(first, 512)], wa_ref.at[core, z, y, :, 256:768]),
+            (store_ref.at[0, :, pl.ds(second, 512)], wb_ref.at[core, z, y]),
+        )
+
+    loads = [
+        pltpu.make_async_copy(source, slot, local_sem.at[i])
+        for i, (source, slot) in enumerate(pieces(y))
+    ]
+    mine = pl.ds(pl.multiple_of((2 * y + t) * HALF, HALF), HALF)
+    x_loads = [
+        pltpu.make_async_copy(
+            turns_ref.at[0, :, b * ROWS : b * ROWS + ROWS], x_ref.at[b, mine], x_local.at[b]
+        )
+        for b in range(BLOCKS)
+    ]
+    for load in loads + x_loads:
+        load.start()
+
+    barrier = pltpu.get_barrier_semaphore()
+    for partner in ((sibling, t), (across, t), (g, 1 - t), (across, 1 - t)):
+        pl.semaphore_signal(barrier, inc=1, device_id=partner, device_id_type=MESH)
+
+    @pl.when(z < LAYERS - 1)
+    def _():
+        pl.semaphore_signal(barrier, inc=1, device_id=(g + 4, t), device_id_type=MESH)
+
+    @pl.when(z > 0)
+    def _():
+        pl.semaphore_signal(barrier, inc=1, device_id=(g - 4, t), device_id_type=MESH)
+
+    pl.semaphore_wait(barrier, 4 + (z + 2) // 3 + (5 - z) // 3)
+
+    def remote(source, slot, send, recv, device):
+        return pltpu.make_async_remote_copy(
+            src_ref=source,
+            dst_ref=slot,
+            send_sem=send,
+            recv_sem=recv,
+            device_id=device,
+            device_id_type=MESH,
+        )
+
+    y_copies = [
+        remote(source, slot, y_send.at[i], y_recv.at[i], (across, t))
+        for i, (source, slot) in enumerate(pieces(1 - y))
+    ]
+
+    def y_arrival(i):
+        slot = (wa_ref.at[core, z, 1 - y, :, 0:256], wa_ref.at[core, z, 1 - y, :, 256:768],
+                wb_ref.at[core, z, 1 - y])[i]
+        return remote(slot, slot, y_send.at[i], y_recv.at[i], (across, t))
+
+    def row_of(h):
+        return y if h == 0 else 1 - y
+
+    def origin(d, k):
+        return z - 1 - k if d == 0 else z + 1 + k
+
+    def arrives(d, k):
+        return z - 1 - k >= 0 if d == 0 else z + 1 + k < LAYERS
+
+    def goes_on(d):
+        return z < LAYERS - 1 if d == 0 else z > 0
+
+    def z_copy(u, d, k, h):
+        slot = weights[u].at[core, origin(d, k - 1), row_of(h)]
+        device = (g + 4, t) if d == 0 else (g - 4, t)
+        return remote(slot, slot, z_send.at[u, d, k, h], z_recv.at[u, d, k, h], device)
+
+    def z_arrival(u, d, k, h):
+        slot = weights[u].at[core, origin(d, k), row_of(h)]
+        device = (g + 4, t) if d == 0 else (g - 4, t)
+        return remote(slot, slot, z_send.at[u, d, k, h], z_recv.at[u, d, k, h], device)
+
+    def sib_copy(u, d, k, h, which):
+        slot = weights[u].at[which, origin(d, k), row_of(h)]
+        j = 0 if k < 0 else 1 + 2 * k + d
+        return remote(slot, slot, sib_send.at[u, j, h], sib_recv.at[u, j, h], (sibling, t))
+
+    def send_home(u, h):
+        for d in range(2):
+
+            @pl.when(goes_on(d))
+            def _():
+                z_copy(u, d, 0, h).start()
+
+        sib_copy(u, 0, -1, h, core).start()
+
+    x_targets = ((g, 1 - t), (across, t), (across, 1 - t))
+    x_copies = [
+        remote(x_ref.at[:, mine], x_ref.at[:, mine], x_send.at[i], x_recv.at[i], device)
+        for i, device in enumerate(x_targets)
+    ]
+
+    def x_arrival(i):
+        spot = ((2 * y + 1 - t), (2 * (1 - y) + t), (2 * (1 - y) + 1 - t))[i]
+        rows = x_ref.at[:, pl.ds(pl.multiple_of(spot * HALF, HALF), HALF)]
+        return remote(rows, rows, x_send.at[i], x_recv.at[i], x_targets[i])
+
+    y_copies[0].start()
+    y_copies[1].start()
+    loads[0].wait()
+    loads[1].wait()
+    send_home(0, 0)
+    y_copies[2].start()
+    for load in x_loads:
+        load.wait()
+    for copy in x_copies:
+        copy.start()
+    loads[2].wait()
+    send_home(1, 0)
+
+    head = pl.ds(pl.multiple_of((2 * t + y) * HEAD_SIZE, HEAD_SIZE), HEAD_SIZE)
+    first = pl.ds(pl.multiple_of(y * 1024, 1024), 512)
+    second = pl.ds(pl.multiple_of(y * 1024 + 512, 512), 512)
+    acca_ref[:, 0:128] = jnp.broadcast_to(key_bias_ref[:, head], (2 * TOKENS, 128))
+    acca_ref[:, 128:256] = jnp.broadcast_to(value_bias_ref[:, head], (2 * TOKENS, 128))
+    acca_ref[:, 256:768] = jnp.broadcast_to(query_bias_ref[:, first], (2 * TOKENS, 512))
+    accb_ref[...] = jnp.broadcast_to(query_bias_ref[:, second], (2 * TOKENS, 512))
+
+    y_arrival(0).wait_recv()
+    y_arrival(1).wait_recv()
+    send_home(0, 1)
+    y_arrival(2).wait_recv()
+    send_home(1, 1)
+
+    def forward(u, k):
+        for h in range(2):
+            for d in range(2):
+
+                @pl.when(arrives(d, k))
+                def _():
+                    z_arrival(u, d, k, h).wait_recv()
+                    if k < LAYERS - 2:
+
+                        @pl.when(goes_on(d))
+                        def _():
+                            z_copy(u, d, k + 1, h).start()
+
+                    sib_copy(u, d, k, h, core).start()
+
+    def add_product(u, layer, row, which):
+        holder = layer * 4 + row * 2 + which
+        accs[u][...] += jnp.dot(
+            x_ref[row_block_ref[holder]],
+            weights[u][which, layer, row],
+            preferred_element_type=jnp.float32,
+        )
+
+    def use(u, k):
+        def both(layer):
+            def body(i, carry):
+                add_product(u, layer, i // 2, lax.rem(i, 2))
+                return carry
+
+            lax.fori_loop(0, 4, body, 0)
+
+        if k < 0:
+            for h in range(2):
+                sib_copy(u, 0, -1, h, other).wait_recv()
+            both(z)
+            return
+        for d in range(2):
+
+            @pl.when(arrives(d, k))
+            def _():
+                for h in range(2):
+                    sib_copy(u, d, k, h, other).wait_recv()
+                both(origin(d, k))
+
+    def rotate(raw):
+        return (raw * cosine_ref[...] + pltpu.roll(raw, 64, 1) * sine_ref[...]).astype(jnp.bfloat16)
+
+    scale = HEAD_SIZE ** (-0.5)
+
+    def rows_of(side):
+        return pl.ds(pl.multiple_of(side * TOKENS, TOKENS), TOKENS)
+
+    def attend(raw, side):
+        query = rotate(raw)
+        parts = []
+        for piece in range(2):
+            low, high = piece * HALF, piece * HALF + HALF
+            scores = (
+                lax.dot_general(
+                    query[low:high],
+                    keys_ref[side, 0:high],
+                    (((1,), (1,)), ((), ())),
+                    preferred_element_type=jnp.float32,
+                )
+                * scale
+            )
+            rows = lax.broadcasted_iota(jnp.int32, (HALF, high), 0) + low
+            cols = lax.broadcasted_iota(jnp.int32, (HALF, high), 1)
+            scores = jnp.where(cols <= rows, scores, -jnp.inf)
+            top = jnp.max(scores, axis=-1, keepdims=True)
+            expd = jnp.exp(scores - top)
+            total = jnp.sum(expd, axis=-1, keepdims=True)
+            shares = (expd / total).astype(jnp.bfloat16)
+            parts.append(
+                jnp.dot(shares, values_ref[side, 0:high], preferred_element_type=jnp.float32)
+            )
+        return parts
+
+    def back_copy(u, p):
+        to = pl.ds(pl.multiple_of(y * 1024 + u * 512 + p * 256, 256), 256)
+        return remote(
+            back_ref.at[u, p], out_ref.at[0, :, to], back_send.at[u, p], back_recv.at[u, p], (across, t)
+        )
+
+    def back_arrival(u, p):
+        to = pl.ds(pl.multiple_of((1 - y) * 1024 + u * 512 + p * 256, 256), 256)
+        return remote(
+            back_ref.at[u, p], out_ref.at[0, :, to], back_send.at[u, p], back_recv.at[u, p], (across, t)
+        )
+
+    length = length_ref[0]
+
+    def attention(u):
+        start = 256 if u == 0 else 0
+        for p in range(2):
+            for e in range(2):
+                lane = start + p * 256 + e * HEAD_SIZE
+                parts = attend(accs[u][rows_of(1 - y), lane : lane + HEAD_SIZE], 1 - y)
+                for piece in range(2):
+                    back_ref[
+                        u, p, piece * HALF : piece * HALF + HALF, e * HEAD_SIZE : e * HEAD_SIZE + HEAD_SIZE
+                    ] = parts[piece].astype(jnp.bfloat16)
+            back_copy(u, p).start()
+        for e in range(4):
+            lane = start + e * HEAD_SIZE
+            parts = attend(accs[u][rows_of(y), lane : lane + HEAD_SIZE], y)
+            to = pl.ds(pl.multiple_of(y * 1024 + u * 512 + e * HEAD_SIZE, HEAD_SIZE), HEAD_SIZE)
+            for piece in range(2):
+                live = lax.broadcasted_iota(jnp.int32, (HALF, HEAD_SIZE), 0) + piece * HALF < length
+                out_ref[0, piece * HALF : piece * HALF + HALF, to] = jnp.where(
+                    live, parts[piece], 0.0
+                ).astype(jnp.bfloat16)
+
+    forward(0, 0)
+    forward(0, 1)
+    forward(1, 0)
+    for i in range(3):
+        x_arrival(i).wait_recv()
+    use(0, -1)
+    use(0, 0)
+    forward(0, 2)
+    use(0, 1)
+    forward(1, 1)
+    use(0, 2)
+    for side in range(2):
+        rows = slice(side * TOKENS, side * TOKENS + TOKENS)
+        keys_ref[side] = rotate(acca_ref[rows, 0:128])
+        values_ref[side] = acca_ref[rows, 128:256].astype(jnp.bfloat16)
+    attention(0)
+    use(1, -1)
+    use(1, 0)
+    use(1, 1)
+    forward(1, 2)
+    use(1, 2)
+    attention(1)
+
+    for u in range(2):
+        for p in range(2):
+            back_arrival(u, p).wait_recv()
+            to = pl.ds(pl.multiple_of((1 - y) * 1024 + u * 512 + p * 256, 256), 256)
+            live = lax.broadcasted_iota(jnp.int32, (TOKENS, 256), 0) < length
+            got = out_ref[0, :, to].astype(jnp.float32)
+            out_ref[0, :, to] = jnp.where(live, got, 0.0).astype(jnp.bfloat16)
+
+    for i in range(3):
+        y_copies[i].wait_send()
+        x_copies[i].wait_send()
+    for u in range(2):
+        for h in range(2):
+            back_copy(u, h).wait_send()
+            sib_copy(u, 0, -1, h, core).wait_send()
+            for d in range(2):
+
+                @pl.when(goes_on(d))
+                def _():
+                    z_copy(u, d, 0, h).wait_send()
+
+                for k in range(LAYERS - 1):
+
+                    @pl.when(arrives(d, k))
+                    def _():
+                        sib_copy(u, d, k, h, core).wait_send()
+                        if k < LAYERS - 2:
+
+                            @pl.when(goes_on(d))
+                            def _():
+                                z_copy(u, d, k + 1, h).wait_send()
+
+
+def rotary_tables():
+    freqs = rotary_base ** (-2.0 * np.arange(64) / HEAD_SIZE)
+    angles = np.arange(TOKENS)[:, None] * freqs[None, :]
+    cosine, sine = np.cos(angles), np.sin(angles)
+    return (
+        np.concatenate([cosine, cosine], axis=1).astype(np.float32),
+        np.concatenate([-sine, sine], axis=1).astype(np.float32),
+    )
+
+
+def per_device_plane(
+    turns,
+    query_store,
+    key_block_holder,
+    value_block_holder,
+    query_bias,
+    key_projection_bias,
+    value_projection_bias,
+    owner,
+    lengths,
+):
+    t = lax.axis_index("tensor")
+    keys_mine = lax.dynamic_slice_in_dim(key_block_holder[0], 2 * t, 2, 1)
+    values_mine = lax.dynamic_slice_in_dim(value_block_holder[0], 2 * t, 2, 1)
+    kv = jnp.concatenate([keys_mine, values_mine], axis=2).reshape(ROWS, 512)
+    numbers = jnp.arange(BLOCKS, dtype=jnp.int32)
+    row_block = jnp.sum(
+        jnp.where(owner[None, :] == numbers[:, None], numbers[None, :], 0), axis=1, dtype=jnp.int32
+    )
+    cosine, sine = rotary_tables()
+    smem = pl.BlockSpec(memory_space=pltpu.SMEM)
+    vmem = pl.BlockSpec(memory_space=pltpu.VMEM)
+    hbm = pl.BlockSpec(memory_space=pl.ANY)
+    return pl.pallas_call(
+        plane_kernel,
+        out_shape=jax.ShapeDtypeStruct((1, TOKENS, 2048), jnp.bfloat16),
+        in_specs=[smem, smem, hbm, hbm, hbm, vmem, vmem, vmem, vmem, vmem],
+        out_specs=vmem,
+        scratch_shapes=[
+            pltpu.VMEM((BLOCKS, 2 * TOKENS, ROWS), jnp.bfloat16),
+            pltpu.VMEM((2, LAYERS, 2, ROWS, WIDTHS[0]), jnp.bfloat16),
+            pltpu.VMEM((2, LAYERS, 2, ROWS, WIDTHS[1]), jnp.bfloat16),
+            pltpu.VMEM((2 * TOKENS, WIDTHS[0]), jnp.float32),
+            pltpu.VMEM((2 * TOKENS, WIDTHS[1]), jnp.float32),
+            pltpu.VMEM((2, TOKENS, HEAD_SIZE), jnp.bfloat16),
+            pltpu.VMEM((2, TOKENS, HEAD_SIZE), jnp.bfloat16),
+            pltpu.VMEM((2, 2, TOKENS, 256), jnp.bfloat16),
+            pltpu.SemaphoreType.DMA((3,)),
+            pltpu.SemaphoreType.DMA((BLOCKS,)),
+            pltpu.SemaphoreType.DMA((3,)),
+            pltpu.SemaphoreType.DMA((3,)),
+            pltpu.SemaphoreType.DMA((3,)),
+            pltpu.SemaphoreType.DMA((3,)),
+            pltpu.SemaphoreType.DMA((2, 2, LAYERS - 1, 2)),
+            pltpu.SemaphoreType.DMA((2, 2, LAYERS - 1, 2)),
+            pltpu.SemaphoreType.DMA((2, 7, 2)),
+            pltpu.SemaphoreType.DMA((2, 7, 2)),
+            pltpu.SemaphoreType.DMA((2, 2)),
+            pltpu.SemaphoreType.DMA((2, 2)),
+        ],
+        compiler_params=pltpu.CompilerParams(
+            collective_id=0, has_side_effects=True, vmem_limit_bytes=48 * 1024 * 1024
+        ),
+    )(
+        row_block,
+        lengths,
+        turns,
+        query_store,
+        kv,
+        query_bias[None],
+        key_projection_bias[None],
+        value_projection_bias[None],
+        jnp.asarray(cosine),
+        jnp.asarray(sine),
+    )
+
+
+def pick(turns, *rest):
+    fits = lax.axis_size("group") == 16 and lax.axis_size("tensor") == 2
+    fits = fits and turns.shape[1:] == (128, 4096)
+    return per_device_plane(turns, *rest) if fits else per_device(turns, *rest)
+
+
 def solution(mesh):
     in_specs = (
         P("group", "tensor", None),
@@ -148,5 +593,5 @@
     )
     out_specs = P("group", None, "tensor")
     return jax.shard_map(
-        per_device, mesh=mesh, in_specs=in_specs, out_specs=out_specs, check_vma=False
-    )
+        pick, mesh=mesh, in_specs=in_specs, out_specs=out_specs, check_vma=False
+    )

time: 279 us -> 108 us (0.39)
  waiting for transfers between devices: 234 us -> 0 us
  Pallas kernels: 0 us -> 102 us
  matrix products: 15.5 us -> 0 us
  between operations: 14.1 us -> 0.82 us
  local copies, waits for them, and re-layouts: 11.3 us -> 4.43 us
  other arithmetic: 3.83 us -> 1.04 us
    all_gather x4 -> x0, waiting for transfers between devices: 234 us -> none  [the longest x1 125 us: per_device(): lax.all_gather(query_store, 'group', axis=0, tiled=True)]
    pallas_call x0 -> x1, Pallas kernels: none -> 102 us  [per_device_plane(): pl.pallas_call(plane_kernel, out_shape=jax.ShapeDtypeStruct((1, TOKENS, 2...]
    dot_general x5 -> x0, matrix products: 15.5 us -> none  [the longest x1 8.24 us: per_device(): jnp.einsum('tgc,gcn->tn', ordered, lax.all_gather(query_store, 'group', a...]
    another operation x1 -> x0, local copies, waits for them, and re-layouts: 2.85 us -> none  [per_device(): gathered.reshape(token_count, group_count, block_rows)]
  transfers between devices with their start and end apart: 4 -> 0, of which waited for: 4 -> 0; matrix products, arithmetic and copies ran while one was open for 5% -> 0% of each run, Pallas kernels for 0% -> 0%
where the time goes in v2:
time: 108 us
  Pallas kernels  102 us (94%)
  local copies, waits for them, and re-layouts  4.43 us (4%)
    pallas_call x1, Pallas kernels, per_device_plane(): pl.pallas_call(plane_kernel, out_shape=jax.ShapeDtypeStruct((1, TOKENS, 2...  102 us
    unnamed x16, local copies, waits for them, and re-layouts  3.12 us

profile of v2, /device:TPU:0, one launch (start us, length us, event | category | flops | bytes accessed | tf_op | source)
XLA Modules:
  0.0 108.1 jit_solution(12671833646347664953)
XLA Ops:
  0.0 0.0 copy-start
  0.7 0.8 select_reduce_fusion.row_block_ref
  1.5 1.3 %dynamic-slice_bitcast_fusion = (bf16[256,2,128]{2,1,0:T(2,128)(2,1)S(1)}, bf16[256,2,128]{2,1,0:T(2,128)(2,1)S(1)}) fusion(bf16[1,256,4,128]{3,2,1,0:T(4,128)(2,1)} %param.14, s32[]{:T(128)S(6)} %select_n.9, bf16[1,256,4,128]{3,2,1,0:T(4,128)(2,1)} %param.13), kind=kLoop, calls=%fused_computation.1 | loop fusion | bytes 524292 | tf_op jit(solution)/shard_map/dynamic_slice | solution.py:522
  2.8 0.3 pad_maximum_fusion
  3.1 0.0 copy-start.2
  3.1 0.0 copy-start.3
  3.1 0.0 copy-start.4
  3.1 0.0 copy-start.5
  3.2 0.0 copy-start.6
  3.2 0.0 copy-done
  3.2 0.8 copy-done.2
  4.0 0.1 copy-done.3
  4.1 0.0 copy-done.4
  4.1 0.0 copy-done.5
  4.1 0.0 copy-done.6
  4.1 0.0 copy-start.1
  4.1 1.2 %copy-done.1 = bf16[1,256,2048]{2,1,0:T(8,128)(2,1)S(1)} copy-done((bf16[1,256,2048]{2,1,0:T(8,128)(2,1)S(1)}, bf16[1,256,2048]{2,1,0:T(8,128)(2,1)}, u32[]{:S(2)}) %copy-start.1) | copy-done | bytes 1048600
  5.3 101.8 %shard_map.109 = bf16[1,256,2048]{2,1,0:T(8,128)(2,1)S(1)} custom-call(s32[16]{0:T(128)S(1)} %select_reduce_fusion.row_block_ref, s32[1]{0:T(128)S(6)} %copy.14.length_ref, bf16[1,128,4096]{2,1,0:T(8,128)(2,1)S(1)} %copy-done, bf16[1,256,2048]{2,1,0:T(8,128)(2,1)S(1)} %copy-done.1, bf16[256,512]{1,0:T(8,128)(2,1)S(1)} %bitcast.9, f32[1,2048]{1,0:T(1,128)S(1)} %bitcast.10, ...), custom_call_target="tpu_custom_call" | custom-call | tf_op jit(solution)/shard_map/pallas_call | solution.py:532
  107.1 1.0 copy.15
  (1 shorter events, 0.0 us)
Async XLA Ops:
  0.0 3.2 %copy-start = (bf16[1,128,4096]{2,1,0:T(8,128)(2,1)S(1)}, bf16[1,128,4096]{2,1,0:T(8,128)(2,1)}, u32[]{:S(2)}) copy-start(bf16[1,128,4096]{2,1,0:T(8,128)(2,1)} %turns_ref.1) | copy-start | bytes 3145732
  3.1 0.9 copy-start.2
  3.1 1.0 copy-start.3
  3.1 1.0 copy-start.4
  3.1 0.9 copy-start.5
  3.2 0.9 copy-start.6
  4.1 1.2 %copy-start.1 = (bf16[1,256,2048]{2,1,0:T(8,128)(2,1)S(1)}, bf16[1,256,2048]{2,1,0:T(8,128)(2,1)}, u32[]{:S(2)}) copy-start(bf16[1,256,2048]{2,1,0:T(8,128)(2,1)} %store_ref.1) | copy-start | bytes 3145732
